TPU v7x, 256 devices: a whole 4x4x8 slice. The times are simulated.
256 devices in a mesh: section: 8 (over x, core), tp: 32 (over y, z).
Axes of the slice: x: 4, y: 4, z: 8, core: 2. Of those that a mesh axis runs over, the one named last changes fastest.
Arguments:
- hidden: bfloat16 [2048, 8192], P(('section', 'tp')), may hold values from -6 to 6
- norm_gain: float32 [8, 8192], P('section'), may hold values from 0.5 to 1.5
- w_query: bfloat16 [8, 8192, 8192], P('section', None, 'tp'), may hold values from -0.125 to 0.125
- w_keyval: bfloat16 [8, 8192, 2048], P('section', None, 'tp'), may hold values from -0.0625 to 0.0625
- w_out: bfloat16 [8, 8192, 8192], P('section', 'tp'), may hold values from -0.25 to 0.25
- kv_pool: bfloat16 [8, 128, 128, 2048], P('section', 'tp'), may hold values from -70 to 70
- page_table: int32 [8, 128], P('section'), may hold values from 0 to 127, as said below
- prefix_len: int32 [8, 4], P('section'), may hold values from 1 to 4096, 10240 in all within a row
- decode_place: int32 [8, 32], P('section'), may hold values from 0 to 31, each once within a row
Outputs:
- handed: bfloat16 [2048, 8192], P(('section', 'tp'))
- decode_cache: bfloat16 [8, 32, 64, 256], P('section', 'tp')
Inputs may be any that keep to these rules, and one draw needn't show every extreme that they name: `page_table`: every page of a section's pool appears once in its page table, and of the pages k * 4 to k * 4 + 3 exactly 1 stand in each request's list. `prefix_len`: some request of every section has exactly 4096 prefix tokens. `decode_place`: every slot appears once for each section.
All inputs are finite; a program needn't handle non-finite values.
Results may differ from a plain program's by a relative error of at most 0.024.
The roundings to bfloat16 on the way count: a program that leaves them out, or rounds other values in their place, can miss the bound.
Values may be sent and summed in bfloat16 or wider, within the bound.
No kernel may reach another device: no remote copies, remote signals or barrier semaphores. Data moves between devices by JAX's collectives and lax.ppermute only.
A program may use at most 128 MiB of HBM per device.

v0:
```python
import jax
import jax.numpy as jnp
from jax import lax
from jax.sharding import PartitionSpec as P

KVH = 8
HD = 128
PAGE = 128
REQ = 4
NEW = 64


rope_theta = 500000.0


def from_behind(value, axis, steps):
    count = lax.axis_size(axis)
    pairs = [(source, (source + steps) % count) for source in range(count)]
    return lax.ppermute(value, axis, pairs)


def rotate(values, positions, dims, apply, head_size):
    rows = values.shape[0]
    cols = values.shape[1]
    inverse = jnp.power(rope_theta, -(dims // 2 * 2).astype(jnp.float32) / head_size)
    angle = positions[:, None].astype(jnp.float32) * inverse[None, :]
    cosine = jnp.cos(angle)[:, 0::2]
    sine = jnp.sin(angle)[:, 0::2]
    pairs = values.reshape(rows, cols // 2, 2)
    even = pairs[:, :, 0]
    odd = pairs[:, :, 1]
    turned = jnp.stack([even * cosine - odd * sine, even * sine + odd * cosine], axis=-1).reshape(
        rows, cols
    )
    return jnp.where(apply[None, :], turned, values)


def attend(qheads, prefix_kv, fresh_kv, lens):
    prefix = prefix_kv.shape[1]
    count = qheads.shape[1]
    scale = HD ** (-0.5)
    score_pre = (
        jnp.einsum(
            "rnhd,rkd->rhnk", qheads, prefix_kv[:, :, :HD], preferred_element_type=jnp.float32
        )
        * scale
    )
    score_new = (
        jnp.einsum(
            "rnhd,rkd->rhnk", qheads, fresh_kv[:, :, :HD], preferred_element_type=jnp.float32
        )
        * scale
    )
    seen_pre = (jnp.arange(prefix, dtype=jnp.int32)[None, :] < lens[:, None])[:, None, None, :]
    npos = jnp.arange(count, dtype=jnp.int32)
    seen_new = (npos[None, :] <= npos[:, None])[None, None, :, :]
    top = jnp.maximum(
        jnp.max(jnp.where(seen_pre, score_pre, -1e30), axis=-1, keepdims=True),
        jnp.max(jnp.where(seen_new, score_new, -1e30), axis=-1, keepdims=True),
    )
    expo_pre = jnp.where(seen_pre, jnp.exp(score_pre - top), 0.0)
    expo_new = jnp.where(seen_new, jnp.exp(score_new - top), 0.0)
    total = jnp.sum(expo_pre, axis=-1, keepdims=True) + jnp.sum(expo_new, axis=-1, keepdims=True)
    weight_pre = (expo_pre / total).astype(jnp.bfloat16)
    weight_new = (expo_new / total).astype(jnp.bfloat16)
    mixed = jnp.einsum(
        "rhnk,rkd->rnhd", weight_pre, prefix_kv[:, :, HD:], preferred_element_type=jnp.float32
    )
    mixed = mixed + jnp.einsum(
        "rhnk,rkd->rnhd", weight_new, fresh_kv[:, :, HD:], preferred_element_type=jnp.float32
    )
    return mixed.astype(jnp.bfloat16)


def local(
    hidden, norm_gain, w_query, w_keyval, w_out, kv_pool, page_table, prefix_len, decode_place
):
    tp_count = lax.axis_size("tp")
    tp_rank = lax.axis_index("tp")
    w_q = w_query[0]
    w_kv = w_keyval[0]
    w_o = w_out[0]
    q_cols = w_q.shape[1]
    kv_cols = w_kv.shape[1]
    rows_dev = hidden.shape[0]
    xf = hidden.astype(jnp.float32)
    meansq = jnp.mean(xf * xf, axis=-1, keepdims=True)
    normed = (xf * lax.rsqrt(meansq + 1e-05) * norm_gain[0][None, :]).astype(jnp.bfloat16)
    piece = lax.all_gather(normed, "tp", axis=0, tiled=True)
    projected = jnp.concatenate(
        [
            jnp.dot(piece, w_q, preferred_element_type=jnp.float32),
            jnp.dot(piece, w_kv, preferred_element_type=jnp.float32),
        ],
        axis=1,
    )
    lens = prefix_len[0]
    positions = (lens[:, None] + jnp.arange(NEW, dtype=jnp.int32)[None, :]).reshape(-1)
    qdims = jnp.arange(q_cols, dtype=jnp.int32)
    query = rotate(projected[:, :q_cols], positions, qdims % HD, qdims >= 0, HD).astype(
        jnp.bfloat16
    )
    kdims = tp_rank * kv_cols + jnp.arange(kv_cols, dtype=jnp.int32)
    keyval = rotate(projected[:, q_cols:], positions, kdims % HD, kdims // HD % 2 == 0, HD).astype(
        jnp.bfloat16
    )
    keyval_all = lax.all_gather(keyval, "tp", axis=1, tiled=True)
    pool_local = kv_pool[0]
    pool_dev = pool_local.shape[0]
    table_flat = page_table[0]
    listed = table_flat.shape[0] // REQ
    prefix = listed * PAGE
    heads_dev = q_cols // HD
    members = tp_count // KVH
    kv_head = tp_rank // members
    by_head = pool_local.reshape(pool_dev, PAGE, KVH, 2 * HD).transpose(2, 0, 1, 3)
    outgoing = jnp.repeat(by_head, members, axis=0)
    received = lax.all_to_all(outgoing, "tp", split_axis=0, concat_axis=0, tiled=True)
    flat_pages = received.reshape(-1, PAGE, 2 * HD)
    prefix_kv = flat_pages[table_flat.reshape(REQ, listed)].reshape(REQ, prefix, 2 * HD)
    fresh_kv = lax.dynamic_slice_in_dim(keyval_all, kv_head * 2 * HD, 2 * HD, 1).reshape(
        REQ, NEW, 2 * HD
    )
    qheads = query.reshape(REQ, NEW, heads_dev, HD)
    attended = attend(qheads, prefix_kv, fresh_kv, lens).reshape(REQ * NEW, q_cols)
    summed = lax.psum(
        jnp.dot(attended, w_o, preferred_element_type=jnp.float32).astype(jnp.bfloat16), "tp"
    ).astype(jnp.float32)
    mine = lax.dynamic_slice_in_dim(summed, tp_rank * rows_dev, rows_dev, 0)
    block = (xf + mine).astype(jnp.bfloat16)
    handed = from_behind(block, "section", 1)
    slots_dev = REQ * KVH // tp_count
    places = decode_place[0]
    units = keyval_all.reshape(REQ, NEW, KVH, 2 * HD)
    unit_ids = jnp.arange(REQ * KVH, dtype=jnp.int32)
    wanted = tp_rank * slots_dev + 0
    unit = jnp.sum(jnp.where(places == wanted, unit_ids, 0))
    request = unit // KVH
    head = unit % KVH
    zero = jnp.zeros((), jnp.int32)
    piece = lax.dynamic_slice(units, (request, zero, head, zero), (1, NEW, 1, 2 * HD))
    pieces = [piece.reshape(NEW, 2 * HD)]
    decode_cache = jnp.stack(pieces, axis=0)[None]
    return (handed, decode_cache)


def solution(mesh):
    placed = (
        P(("section", "tp"), None),
        P("section", None),
        P("section", None, "tp"),
        P("section", None, "tp"),
        P("section", "tp", None),
        P("section", "tp", None, None),
        P("section", None),
        P("section", None),
        P("section", None),
    )
    return jax.shard_map(
        local,
        mesh=mesh,
        in_specs=placed,
        out_specs=(P(("section", "tp"), None), P("section", "tp", None, None)),
        check_vma=False,
    )
```

profile of v0, /device:TPU:1, one launch (start us, length us, event | category | flops | bytes accessed | tf_op | source)
XLA Modules:
  0.0 479.9 jit_solution(14386699679263942490)
XLA Ops:
  7.2 2.4 copy.52
  10.2 4.3 broadcast_in_dim.75
  14.5 12.3 %all-to-all-start = ((bf16[32,4,128,256]{3,2,1,0:T(8,128)(2,1)}), bf16[32,4,128,256]{3,2,1,0:T(8,128)(2,1)}, u32[]{:S(2)}, u32[]{:S(2)}) async-start(bf16[32,4,128,256]{3,2,1,0:T(8,128)(2,1)} %bitcast.135), calls=%async_computation | async-start | bytes 16777216 | tf_op jit(solution)/shard_map/all_to_all | solution.py:118
  27.0 0.8 fusion.18
  29.8 1.0 multiply_sine_fusion
  30.8 4.5 slice.41
  35.3 4.5 slice.39
  39.8 6.4 %copy.32 = bf16[256,8192]{1,0:T(8,128)(2,1)} copy(bf16[256,8192]{0,1:T(8,128)(2,1)} %bitcast.141) | data formatting | bytes 8388608 | tf_op jit(solution)/shard_map/dot_general | solution.py:92
  46.2 7.7 %dot_general.26 = bf16[128,2,8192]{2,1,0:T(2,128)(2,1)} reshape(bf16[256,8192]{1,0:T(8,128)(2,1)} %copy.32) | data formatting | bytes 8388608 | tf_op jit(solution)/shard_map/dot_general | solution.py:92
  53.9 120.2 %all-gather.3.cloned.1.call-done = bf16[256,8192]{1,0:T(8,128)(2,1)} async-done(((bf16[8,8192]{1,0:T(8,128)(2,1)}), bf16[256,8192]{1,0:T(8,128)(2,1)}) %all-gather.3.cloned.1.call-update) | async-done | bytes 4194320 | tf_op jit(solution)/shard_map/all_gather | solution.py:89
  174.1 3.6 fusion.14
  178.0 0.7 select_convert_fusion
  179.0 8.5 %fusion.7 = f32[256,128,2]{1,0,2:T(8,128)S(1)} fusion(bf16[256,8192]{1,0:T(8,128)(2,1)} %all-gather.3.cloned.1.call-done, bf16[128,2,8192]{2,1,0:T(2,128)(2,1)} %dot_general.26), kind=kOutput, calls=%fused_computation.14 | convolution fusion | flops 1073741824 | bytes 8650752 | tf_op jit(solution)/shard_map/dot_general | solution.py:92
  188.2 85.3 %all-gather.5.cloned.1.call-done = bf16[256,2048]{0,1:T(8,128)(2,1)} async-done(((bf16[256,64]{0,1:T(8,128)(2,1)}), bf16[256,2048]{0,1:T(8,128)(2,1)}) %all-gather.5.cloned.1.call-update) | async-done | bytes 1048592 | tf_op jit(solution)/shard_map/all_gather | solution.py:107
  273.5 0.9 constant_dynamic-slice_fusion.1
  274.8 10.2 %gather_fusion = bf16[128,128,256]{2,1,0:T(8,128)(2,1)} fusion(bf16[128,128,256]{2,1,0:T(8,128)(2,1)} %bitcast.2, s32[1024]{0:T(1024)S(1)} %pad_clamp_fusion), kind=kCustom, calls=%fused_computation | custom fusion | bytes 16777728 | tf_op jit(solution)/shard_map/gather | solution.py:120
  285.0 3.8 fusion
  288.9 2.2 fusion.3
  291.1 2.9 fusion.5
  294.4 3.3 convolution_convert_fusion
  297.7 163.8 %all-reduce.2.cloned.1.call-done = bf16[256,8192]{1,0:T(8,128)(2,1)} async-done(((bf16[256,8192]{1,0:T(8,128)(2,1)}), bf16[256,8192]{1,0:T(8,128)(2,1)}) %all-reduce.2.cloned.1.call-update) | async-done | bytes 4194320 | tf_op jit(solution)/shard_map/psum | solution.py:126
  461.6 0.9 fusion.19
  462.5 4.4 collective-permute-start
  470.2 1.5 copy.43
  (73 shorter events, 7.2 us)
Async XLA Ops:
  7.2 166.9 %copy-start = (bf16[1,8192,64]{1,2,0:T(8,128)(2,1)S(1)}, bf16[1,8192,64]{1,2,0:T(8,128)(2,1)}, u32[]{:S(2)}) copy-start(bf16[1,8192,64]{1,2,0:T(8,128)(2,1)} %param.12) | copy-start | bytes 3145732
  14.4 12.4 %copy-start.3 = (bf16[8,8192]{1,0:T(8,128)(2,1)S(1)}, bf16[8,8192]{1,0:T(8,128)(2,1)}, u32[]{:S(2)}) copy-start(bf16[8,8192]{1,0:T(8,128)(2,1)} %param.9) | copy-start | bytes 393220
  14.4 12.6 %copy-start.4 = (f32[1,8192]{1,0:T(1,128)S(1)}, f32[1,8192]{1,0:T(1,128)}, u32[]{:S(2)}) copy-start(f32[1,8192]{1,0:T(1,128)} %param.10) | copy-start | bytes 98308
  14.4 13.9 %copy-start.6 = (s32[1,128]{1,0:T(1,128)S(1)}, s32[1,128]{1,0:T(1,128)}, u32[]{:S(2)}) copy-start(s32[1,128]{1,0:T(1,128)} %param.15) | copy-start | bytes 1540
  14.4 14.8 %copy-start.5 = (s32[1,4]{1,0:T(1,128)S(1)}, s32[1,4]{1,0:T(1,128)}, u32[]{:S(2)}) copy-start(s32[1,4]{1,0:T(1,128)} %param.16) | copy-start | bytes 52
  14.5 260.3 %all-to-all-start = ((bf16[32,4,128,256]{3,2,1,0:T(8,128)(2,1)}), bf16[32,4,128,256]{3,2,1,0:T(8,128)(2,1)}, u32[]{:S(2)}, u32[]{:S(2)}) async-start(bf16[32,4,128,256]{3,2,1,0:T(8,128)(2,1)} %bitcast.135), calls=%async_computation | async-start | bytes 16777216 | tf_op jit(solution)/shard_map/all_to_all | solution.py:118
  26.8 147.3 %all-gather.3.cloned.1.call-start = ((), (), s32[]{:S(2)}) async-start(), calls=%async_computation.1 | async-start | bytes 4325376 | tf_op jit(solution)/shard_map/all_gather | solution.py:89
  27.8 245.7 %all-gather.5.cloned.1.call-start = ((), (), s32[]{:S(2)}) async-start(), calls=%async_computation.2 | async-start | bytes 1081344 | tf_op jit(solution)/shard_map/all_gather | solution.py:107
  178.7 282.9 %all-reduce.2.cloned.1.call-start = ((), (), s32[]{:S(2)}) async-start(), calls=%async_computation.3 | async-start | bytes 8388608 | tf_op jit(solution)/shard_map/psum | solution.py:126
  285.0 6.1 %slice-start = ((s8[8388608]{0:T(1024)(128)(4,1)}), s8[4194304]{0:T(1024)(128)(4,1)S(1)}, s32[]{:S(2)}) async-start(s8[8388608]{0:T(1024)(128)(4,1)} %bitcast.137), calls=%async_computation.4 | async-start | bytes 8388608
  285.0 6.1 %slice-start.1 = ((s8[8388608]{0:T(1024)(128)(4,1)}), s8[4194304]{0:T(1024)(128)(4,1)S(1)}, s32[]{:S(2)}) async-start(s8[8388608]{0:T(1024)(128)(4,1)} %bitcast.137), calls=%async_computation.5 | async-start | bytes 8388608
  291.1 3.3 copy-start.2
  294.0 172.9 %copy-start.7 = (s32[1,32]{1,0:T(1,128)S(1)}, s32[1,32]{1,0:T(1,128)}, u32[]{:S(2)}) copy-start(s32[1,32]{1,0:T(1,128)} %param.17) | copy-start | bytes 388
  294.4 178.9 %copy-start.1 = (bf16[1,8192,64]{1,2,0:T(8,128)(2,1)S(1)}, bf16[1,8192,64]{1,2,0:T(8,128)(2,1)}, u32[]{:S(2)}) copy-start(bf16[1,8192,64]{1,2,0:T(8,128)(2,1)} %param.12) | copy-start | bytes 3145732
  462.5 10.2 %collective-permute-start = (bf16[8,8192]{1,0:T(8,128)(2,1)S(1)}, bf16[8,8192]{1,0:T(8,128)(2,1)S(1)}, u32[]{:S(2)}, u32[]{:S(2)}) collective-permute-start(bf16[8,8192]{1,0:T(8,128)(2,1)S(1)} %fusion.19), channel_id=1, source_target_pairs={{0,32},{32,64},{64,96},{96,128},{128,160},{160,192},{192,224},{224... | collective-permute-start | bytes 393224 | tf_op jit(solution)/shard_map/ppermute | solution.py:19
Sparse Core Ops, SparseCore 0:
  30.8 143.2 all-gather.2
  178.8 94.6 all-gather.4
  297.9 163.6 all-reduce.1
where the time goes:
time: 480 us
  waiting for transfers between devices  369 us (77%)
  local copies, waits for them, and re-layouts  46.3 us (10%)
  matrix products  22.6 us (5%)
  starting transfers between devices  17 us (4%)
  between operations  16.7 us (3%)
  other arithmetic  7.85 us (2%)
    psum x1, waiting for transfers between devices, local(): lax.psum(jnp.dot(attended, w_o, preferred_element_type=jnp.float32).astyp...  164 us
    all_gather x1, waiting for transfers between devices, local(): piece = lax.all_gather(normed, 'tp', axis=0, tiled=True)  120 us
    all_gather x1, waiting for transfers between devices, local(): keyval_all = lax.all_gather(keyval, 'tp', axis=1, tiled=True)  85.3 us
    dot_general x2, local copies, waits for them, and re-layouts, local(): jnp.dot(piece, w_q, preferred_element_type=jnp.float32)  14 us
    all_to_all x1, starting transfers between devices, local(): lax.all_to_all(outgoing, 'tp', split_axis=0, concat_axis=0, tiled=True)  12.3 us
    gather x1, local copies, waits for them, and re-layouts, local(): flat_pages[table_flat.reshape(REQ, listed)].reshape(REQ, prefix, 2 * HD)  10.2 us
  transfers between devices with their start and end apart: 5, of which 3 were waited for; matrix products, arithmetic and copies ran while one was open for 9% of the time, Pallas kernels for 0%

commit v1 on v0

v1 whole, which is shorter than its diff:
```python
import functools

import jax
import jax.numpy as jnp
from jax import lax
from jax.experimental import pallas as pl
from jax.experimental.pallas import tpu as pltpu
from jax.sharding import Mesh, PartitionSpec as P

D = 8192
KVH = 8
HD = 128
PAGE = 128
REQ = 4
NEW = 64
NY = 4
NZ = 8
NTP = 32
QC = 256
GROUP = 8

rope_theta = 500000.0
f32 = jnp.float32
bf16 = jnp.bfloat16
VMEM_LIMIT = 60 * 1024 * 1024


def shift(value, axis, steps):
    count = lax.axis_size(axis)
    return lax.ppermute(value, axis, [(i, (i + steps) % count) for i in range(count)])


def shift_quad(value, steps):
    pairs = [(q * 4 + i, q * 4 + (i + steps) % 4) for q in range(2) for i in range(4)]
    return lax.ppermute(value, "z", pairs)


def regroup_kernel(order_ref, place_ref, pool_ref, *outs):
    for k, out in enumerate(outs):
        first = lax.rem(place_ref[0] + k, NY) * (4 * HD)
        for h in range(2):
            at = pl.multiple_of(first + h * 2 * HD, 2 * HD)
            out[h, 0] = pool_ref[0, :, pl.ds(at, 2 * HD)]


def regroup(pool, order, place):
    out = pl.BlockSpec((2, 1, PAGE, 2 * HD), lambda r, order, place: (0, r, 0, 0))
    return pl.pallas_call(
        regroup_kernel,
        grid_spec=pltpu.PrefetchScalarGridSpec(
            num_scalar_prefetch=2,
            grid=(REQ,),
            in_specs=[
                pl.BlockSpec((1, PAGE, 2 * KVH * HD), lambda r, order, place: (order[r], 0, 0))
            ],
            out_specs=[out] * NY,
        ),
        out_shape=[jax.ShapeDtypeStruct((2, REQ, PAGE, 2 * HD), bf16)] * NY,
    )(order, place, pool)


Z_ORDER = (0, -1, 1, -2, 2, -3, 3, -4)
Y_ORDER = (0, -1, 1, -2)


def project_kernel(
    place_ref,
    x0,
    x1,
    x2,
    x3a,
    x3b,
    wq,
    wkv,
    cosine,
    sine,
    cosine_kv,
    sine_kv,
    o0,
    o1,
    o2,
    o3,
    acc,
    turned,
    ready,
):
    step = pl.program_id(0)
    rows = jnp.concatenate([x0[...], x1[...], x2[...], x3a[...], x3b[...]], axis=0)
    part_q = jnp.dot(rows, wq[...], preferred_element_type=f32)
    part_kv = jnp.dot(rows, wkv[...], preferred_element_type=f32)

    @pl.when(step == 0)
    def _():
        acc[:, :QC] = part_q
        acc[:, QC:] = part_kv

    @pl.when(step > 0)
    def _():
        acc[:, :QC] += part_q
        acc[:, QC:] += part_kv

    @pl.when(step == pl.num_programs(0) - 1)
    def _():
        for k in range(NY):
            for j in range(NZ):
                yk = lax.rem(place_ref[0] + (Y_ORDER[k] + NY), NY)
                zj = lax.rem(place_ref[1] + (Z_ORDER[j] + NZ), NZ)
                at = pl.multiple_of(yk * 64 + zj * 8, 8)
                turned[pl.ds(at, 8), :] = acc[k * 64 + j * 8 : k * 64 + j * 8 + 8, :]
        even = lax.broadcasted_iota(jnp.int32, (REQ * NEW, HD), 1) % 2 == 0
        for c in range(3):
            v = turned[:, c * HD : (c + 1) * HD]
            cs, sn = (cosine, sine) if c < 2 else (cosine_kv, sine_kv)
            other = jnp.where(even, -pltpu.roll(v, HD - 1, 1), pltpu.roll(v, 1, 1))
            done = (v * cs[...] + other * sn[...]).astype(bf16)
            for r in range(REQ):
                ready[r, :, c * HD : (c + 1) * HD] = done[r * NEW : (r + 1) * NEW]
        for k, out in enumerate((o0, o1, o2, o3)):
            out[...] = ready[lax.rem(place_ref[2] + k, REQ)]


def project(place, pieces, wq, wkv, tables):
    kc = 1024
    rows = [p.shape[0] for p in pieces]
    whole = pl.BlockSpec((REQ * NEW, HD), lambda k, p: (0, 0))
    return pl.pallas_call(
        project_kernel,
        grid_spec=pltpu.PrefetchScalarGridSpec(
            num_scalar_prefetch=1,
            grid=(D // kc,),
            in_specs=[pl.BlockSpec((r, kc), lambda k, p: (0, k)) for r in rows]
            + [
                pl.BlockSpec((kc, QC), lambda k, p: (k, 0)),
                pl.BlockSpec((kc, HD), lambda k, p: (k, 0)),
            ]
            + [whole] * 4,
            out_specs=[pl.BlockSpec((NEW, QC + HD), lambda k, p: (0, 0))] * REQ,
            scratch_shapes=[
                pltpu.VMEM((REQ * NEW, QC + HD), f32),
                pltpu.VMEM((REQ * NEW, QC + HD), f32),
                pltpu.VMEM((REQ, NEW, QC + HD), bf16),
            ],
        ),
        out_shape=[jax.ShapeDtypeStruct((NEW, QC + HD), bf16)] * REQ,
        compiler_params=pltpu.CompilerParams(vmem_limit_bytes=VMEM_LIMIT),
    )(place, *pieces, wq, wkv, *tables)


CARRY = NEW * 2 * HD // 8


CHUNK = 4


def attend_kernel(info_ref, p0, p1, p2, p3, kv_ref, o0, o1, o2, o3, unit_ref, q_s, s_s, fresh):
    pieces = (p0, p1, p2, p3)
    member = info_ref[0]
    length = info_ref[1]
    for k in range(4):
        for h in range(2):
            row = (k * 2 + h) * NEW
            q_s[row : row + NEW, :] = pieces[k][:, h * HD : (h + 1) * HD]
        fresh[k] = pieces[k][:, QC:].astype(f32)
    key_new = fresh[lax.rem(member, 4)] + fresh[lax.rem(member + 3, 4)]
    val_new = fresh[lax.rem(member + 2, 4)] + fresh[lax.rem(member + 1, 4)]
    for a in range(8):
        at = a * 2 * HD
        rows = slice(a * 8, a * 8 + 8)
        unit_ref[:, at : at + HD] = key_new[rows].astype(bf16)
        unit_ref[:, at + HD : at + 2 * HD] = val_new[rows].astype(bf16)
    key_new, val_new = key_new.astype(bf16), val_new.astype(bf16)
    q = q_s[...]
    rows = GROUP * NEW
    nt = (((1,), (1,)), ((), ()))
    s_new = lax.dot_general(q, key_new, nt, preferred_element_type=f32)
    token = lax.broadcasted_iota(jnp.int32, (rows, NEW), 0) % NEW
    s_new = jnp.where(lax.broadcasted_iota(jnp.int32, (rows, NEW), 1) <= token, s_new, -1e30)
    top = jnp.full((rows, HD), -1e30, f32)
    lane = lax.broadcasted_iota(jnp.int32, (1, HD), 1)
    width = CHUNK * PAGE
    for c in range(NTP // CHUNK):
        keys = kv_ref[c * CHUNK : (c + 1) * CHUNK, :, :HD].reshape(width, HD)
        s = lax.dot_general(q, keys, nt, preferred_element_type=f32)
        for o in range(CHUNK):
            start = info_ref[2 + c * CHUNK + o] * PAGE
            part = jnp.where(lane < length - start, s[:, o * PAGE : (o + 1) * PAGE], -1e30)
            s_s[:, c * width + o * PAGE : c * width + (o + 1) * PAGE] = part
            top = jnp.maximum(top, part)
    m = jnp.maximum(
        jnp.max(top, axis=1, keepdims=True), jnp.max(s_new, axis=1, keepdims=True)
    )
    factor = HD ** (-0.5) * 1.4426950408889634
    e_new = jnp.exp2((s_new - m) * factor)
    total = jnp.zeros((rows, HD), f32)
    for c in range(NTP):
        e = jnp.exp2((s_s[:, c * PAGE : (c + 1) * PAGE] - m) * factor)
        s_s[:, c * PAGE : (c + 1) * PAGE] = e
        total = total + e
    inverse = 1.0 / (
        jnp.sum(total, axis=1, keepdims=True) + jnp.sum(e_new, axis=1, keepdims=True)
    )
    mixed = jnp.dot((e_new * inverse).astype(bf16), val_new, preferred_element_type=f32)
    for c in range(NTP // CHUNK):
        vals = kv_ref[c * CHUNK : (c + 1) * CHUNK, :, HD:].reshape(width, HD)
        w = (s_s[:, c * width : (c + 1) * width] * inverse).astype(bf16)
        mixed = mixed + jnp.dot(w, vals, preferred_element_type=f32)
    mixed = mixed.astype(bf16)
    for k, out in enumerate((o0, o1, o2, o3)):
        for h in range(2):
            row = (k * 2 + h) * NEW
            out[:, h * HD : (h + 1) * HD] = mixed[row : row + NEW]


def attend(info, pieces, kv):
    vm = pl.BlockSpec(memory_space=pltpu.VMEM)
    return pl.pallas_call(
        attend_kernel,
        in_specs=[pl.BlockSpec(memory_space=pltpu.SMEM)] + [vm] * 5,
        out_specs=[vm] * 5,
        out_shape=[jax.ShapeDtypeStruct((NEW, QC), bf16)] * 4
        + [jax.ShapeDtypeStruct((8, CARRY), bf16)],
        scratch_shapes=[
            pltpu.VMEM((GROUP * NEW, HD), bf16),
            pltpu.VMEM((GROUP * NEW, NTP * PAGE), f32),
            pltpu.VMEM((4, NEW, HD), f32),
        ],
        compiler_params=pltpu.CompilerParams(vmem_limit_bytes=VMEM_LIMIT),
    )(info, *pieces, kv)


OUT_COLS = 2048


def outward_kernel(place_ref, a0, a1, a2, a3, wo, o0, o1, o2, o3, rows):
    @pl.when(pl.program_id(0) == 0)
    def _():
        for k, piece in enumerate((a0, a1, a2, a3)):
            at = lax.rem(place_ref[2] + k + 4 - place_ref[0], 4)
            rows[pl.ds(pl.multiple_of(at * NEW, NEW), NEW), :] = piece[...]

    part = jnp.dot(rows[...], wo[...], preferred_element_type=f32).astype(bf16)
    for j, out in enumerate((o0, o1, o2, o3)):
        out[...] = part[j * NEW : (j + 1) * NEW]


def outward(place, pieces, wo, first, cols):
    steps = cols // OUT_COLS
    lead = first // OUT_COLS
    return pl.pallas_call(
        outward_kernel,
        grid_spec=pltpu.PrefetchScalarGridSpec(
            num_scalar_prefetch=1,
            grid=(steps,),
            in_specs=[pl.BlockSpec((NEW, QC), lambda n, p: (0, 0))] * 4
            + [pl.BlockSpec((QC, OUT_COLS), lambda n, p: (0, n + lead))],
            out_specs=[pl.BlockSpec((NEW, OUT_COLS), lambda n, p: (0, n))] * 4,
            scratch_shapes=[pltpu.VMEM((REQ * NEW, QC), bf16)],
        ),
        out_shape=[jax.ShapeDtypeStruct((NEW, cols), bf16)] * 4,
        compiler_params=pltpu.CompilerParams(vmem_limit_bytes=VMEM_LIMIT),
    )(place, *pieces, wo)


def gather_kernel(pick_ref, b0, b1, b2, *rest):
    total = b0[...].astype(f32) + b1[...].astype(f32) + b2[...].astype(f32)
    cols = total.shape[1]
    out_ref = rest[NY] if len(rest) > 1 else rest[0]
    for k in range(NZ):
        out_ref[k, :, :cols] = total[k * 8 : k * 8 + 8].astype(bf16)
    if len(rest) > 1:
        units = rest[NY + 1]
        for k in range(NY):
            units[k] = rest[k][...]
        for k in range(NZ):
            out_ref[k, :, cols:] = units[pick_ref[k]]


def gather_blocks(pick, blocks, units):
    cols = blocks[0].shape[1] + (CARRY if units else 0)
    vm = pl.BlockSpec(memory_space=pltpu.VMEM)
    return pl.pallas_call(
        gather_kernel,
        in_specs=[pl.BlockSpec(memory_space=pltpu.SMEM)] + [vm] * (3 + len(units)),
        out_specs=vm,
        out_shape=jax.ShapeDtypeStruct((NZ, 8, cols), bf16),
        scratch_shapes=[pltpu.VMEM((NY, 8, CARRY), bf16)] if units else [],
        compiler_params=pltpu.CompilerParams(vmem_limit_bytes=VMEM_LIMIT),
    )(pick, *blocks, *units)


def sum_over_y(blocks):
    half = blocks[2].shape[1] // 2
    right = shift(blocks[2][:, :half], "y", 1)
    left = shift(blocks[2][:, half:], "y", -1)
    none = jnp.zeros((NEW, half), f32)
    to_right = blocks[1].astype(f32) + jnp.concatenate([right.astype(f32), none], axis=1)
    to_left = blocks[3].astype(f32) + jnp.concatenate([none, left.astype(f32)], axis=1)
    return (
        blocks[0],
        shift(to_right.astype(bf16), "y", 1),
        shift(to_left.astype(bf16), "y", -1),
    )


def to_next(value):
    return shift(value, "section", 1)


def local(
    hidden, norm_gain, w_query, w_keyval, w_out, kv_pool, page_table, prefix_len, decode_place
):
    y = lax.axis_index("y")
    z = lax.axis_index("z")
    rank = y * NZ + z
    member = rank % 4
    place = jnp.stack([y, z, member]).astype(jnp.int32)
    lens = prefix_len[0]
    table = page_table[0].reshape(REQ, -1)

    order = jnp.sum(jnp.where(table // 4 == rank, table % 4, 0), axis=1).astype(jnp.int32)
    toward = [t.reshape(NZ, PAGE, 2 * HD) for t in regroup(kv_pool[0], order, place)]
    column = [toward[0]] + [shift(toward[k], "y", k) for k in range(1, NY)]

    xf = hidden.astype(f32)
    meansq = jnp.mean(xf * xf, axis=-1, keepdims=True)
    normed = (xf * lax.rsqrt(meansq + 1e-05) * norm_gain[0][None, :]).astype(bf16)
    half = D // 2
    r1, l1 = shift(normed, "z", 1), shift(normed, "z", -1)
    r2, l2 = shift(r1, "z", 1), shift(l1, "z", -1)
    r3, l3 = shift(r2, "z", 1), shift(l2, "z", -1)
    r4, l4 = shift(r3[:, :half], "z", 1), shift(l3[:, half:], "z", -1)
    mine = jnp.concatenate([normed, r1, l1, r2, l2, r3, l3, jnp.concatenate([r4, l4], 1)], 0)
    *column, mine = lax.optimization_barrier((*column, mine))
    kv = lax.all_to_all(jnp.stack(column, axis=1), "z", split_axis=0, concat_axis=0, tiled=True)
    kv = kv.reshape(NTP, PAGE, 2 * HD)
    yr1, yl1 = shift(mine, "y", 1), shift(mine, "y", -1)
    yr2, yl2 = shift(yr1[:32], "y", 1), shift(yl1[32:], "y", -1)

    dims = jnp.arange(HD, dtype=jnp.int32)
    positions = (lens[:, None] + jnp.arange(NEW, dtype=jnp.int32)[None, :]).reshape(-1)
    inverse = jnp.power(rope_theta, -(dims // 2 * 2).astype(f32) / HD)
    angle = positions[:, None].astype(f32) * inverse[None, :]
    cosine, sine = jnp.cos(angle), jnp.sin(angle)
    is_key = member < 2
    tables = (cosine, sine, jnp.where(is_key, cosine, 1.0), jnp.where(is_key, sine, 0.0))
    wkv = w_keyval[0]
    zero = jnp.zeros_like(wkv)
    odd = member % 2 == 1
    wkv = jnp.concatenate([jnp.where(odd, zero, wkv), jnp.where(odd, wkv, zero)], axis=1)
    projected = project(place, (mine, yr1, yl1, yr2, yl2), w_query[0], wkv, tables)

    got = [projected[0]] + [shift_quad(projected[k], k) for k in (1, 2, 3)]
    my_table = lax.dynamic_index_in_dim(table, member, 0, keepdims=False)
    owners = jnp.arange(NTP, dtype=jnp.int32)
    owners = (y - owners % NY) % NY * NZ + owners // NY
    starts = jnp.sum(
        jnp.where(my_table[None, :] // 4 == owners[:, None], jnp.arange(NTP)[None, :], 0), axis=1
    )
    my_len = jnp.sum(jnp.where(jnp.arange(REQ) == member, lens, 0))
    info = jnp.concatenate([jnp.stack([member, my_len]), starts]).astype(jnp.int32)
    *attended, unit = attend(info, got, kv)
    back = [attended[0]] + [shift_quad(attended[k], -k) for k in (1, 2, 3)]

    places = decode_place[0]
    slots = y * NZ + jnp.arange(NZ, dtype=jnp.int32)
    unit_ids = jnp.arange(REQ * KVH, dtype=jnp.int32)
    held = jnp.sum(jnp.where(places[None, :] == slots[:, None], unit_ids[None, :], 0), axis=1)
    holder = held % KVH * 4 + held // KVH
    pick = (y - holder // NZ) % NY
    units = [unit] + [shift(unit, "y", k) for k in (1, 2, 3)]

    parts = []
    for first in range(0, D, D // 2):
        blocks = outward(place, back, w_out[0], first, D // 2)
        sums = gather_blocks(pick.astype(jnp.int32), sum_over_y(blocks), units)
        units = []
        parts.append(lax.all_to_all(sums, "z", split_axis=0, concat_axis=0, tiled=True))
    summed = jnp.concatenate(
        [jnp.sum(p[:, :, : D // 2].astype(f32), axis=0) for p in parts], axis=1
    )
    handed = to_next((xf + summed).astype(bf16))
    wanted = jnp.sum(jnp.where(places == rank, unit_ids, 0))
    from_z = (wanted % KVH * 4 + wanted // KVH) % NZ
    decode_cache = lax.dynamic_index_in_dim(parts[0][:, :, D // 2 :], from_z, 0, keepdims=False)
    decode_cache = decode_cache.reshape(8, 8, 2 * HD).transpose(1, 0, 2)
    return handed, decode_cache.reshape(1, 1, NEW, 2 * HD)


def solution(mesh):
    names = ("section", "y", "z")
    tp = ("y", "z")
    grid = Mesh(mesh.devices.reshape(mesh.devices.shape[0], NY, NZ), names)
    placed = (
        P(names, None),
        P("section", None),
        P("section", None, tp),
        P("section", None, tp),
        P("section", tp, None),
        P("section", tp, None, None),
        P("section", None),
        P("section", None),
        P("section", None),
    )
    return jax.shard_map(
        local,
        mesh=grid,
        in_specs=placed,
        out_specs=(P(names, None), P("section", tp, None, None)),
        check_vma=False,
    )
```

time: 480 us -> 215 us (0.45)
  waiting for transfers between devices: 369 us -> 65.4 us
  starting transfers between devices: 17 us -> 80.5 us
  local copies, waits for them, and re-layouts: 46.3 us -> 10.5 us
  Pallas kernels: 0 us -> 35.6 us
  matrix products: 22.6 us -> 0 us
  between operations: 16.7 us -> 3.61 us
  other arithmetic: 7.85 us -> 17.8 us
    all_gather x2 -> x0, waiting for transfers between devices: 206 us -> none  [the longest x1 120 us: local(): piece = lax.all_gather(normed, 'tp', axis=0, tiled=True)]
    psum x1 -> x0, waiting for transfers between devices: 164 us -> none  [local(): lax.psum(jnp.dot(attended, w_o, preferred_element_type=jnp.float32).astyp...]
    ppermute x1 -> x33, starting transfers between devices: 4.4 us -> 64 us  [the longest x27 57.3 us: shift(): lax.ppermute(value, axis, [(i, (i + steps) % count) for i in range(count)])]
    ppermute x1 -> x33, waiting for transfers between devices: 0.01 us -> 52 us  [the longest x27 45.5 us: shift(): lax.ppermute(value, axis, [(i, (i + steps) % count) for i in range(count)])]
    pallas_call x0 -> x7, Pallas kernels: none -> 35.6 us  [the longest x1 10 us: project(): pl.pallas_call(project_kernel, grid_spec=pltpu.PrefetchScalarGridSpec(num...]
    dot_general x7 -> x0, matrix products: 22.6 us -> none  [the longest x1 8.52 us: local(): jnp.dot(piece, w_q, preferred_element_type=jnp.float32)]
    dot_general x2 -> x0, local copies, waits for them, and re-layouts: 14 us -> none  [local(): jnp.dot(piece, w_q, preferred_element_type=jnp.float32)]
    all_to_all x1 -> x3, waiting for transfers between devices: 0.01 us -> 13.3 us  [the longest x2 13.3 us: local(): lax.all_to_all(sums, 'z', split_axis=0, concat_axis=0, tiled=True)]
  transfers between devices with their start and end apart: 5 -> 36, of which waited for: 3 -> 16; matrix products, arithmetic and copies ran while one was open for 9% -> 8% of each run, Pallas kernels for 0% -> 11%
where the time goes in v1:
time: 215 us; the launch traced here: 213 us
  starting transfers between devices  80.5 us (37%)
  waiting for transfers between devices  65.4 us (30%)
  Pallas kernels  35.6 us (17%)
  other arithmetic  17.8 us (8%)
  local copies, waits for them, and re-layouts  10.5 us (5%)
  between operations  3.61 us (2%)
    ppermute x27, starting transfers between devices, shift(): lax.ppermute(value, axis, [(i, (i + steps) % count) for i in range(count)])  57.3 us
    ppermute x27, waiting for transfers between devices, shift(): lax.ppermute(value, axis, [(i, (i + steps) % count) for i in range(count)])  45.5 us
    all_to_all x2, waiting for transfers between devices, local(): lax.all_to_all(sums, 'z', split_axis=0, concat_axis=0, tiled=True)  13.3 us
    all_to_all x2, starting transfers between devices, local(): lax.all_to_all(sums, 'z', split_axis=0, concat_axis=0, tiled=True)  11.3 us
    pallas_call x1, Pallas kernels, project(): pl.pallas_call(project_kernel, grid_spec=pltpu.PrefetchScalarGridSpec(num...  10 us
    pallas_call x1, Pallas kernels, attend(): pl.pallas_call(attend_kernel, in_specs=[pl.BlockSpec(memory_space=pltpu.S...  8.4 us
    pallas_call x2, Pallas kernels, outward(): pl.pallas_call(outward_kernel, grid_spec=pltpu.PrefetchScalarGridSpec(num...  7.58 us
    unnamed x65, local copies, waits for them, and re-layouts  7.41 us
  transfers between devices with their start and end apart: 36, of which 16 were waited for; matrix products, arithmetic and copies ran while one was open for 8% of the time, Pallas kernels for 11%

profile of v1, /device:TPU:1, one launch (start us, length us, event | category | flops | bytes accessed | tf_op | source)
XLA Modules:
  0.0 213.3 jit_solution(6579898678712088580)
XLA Ops:
  5.3 4.0 %collective-permute-start.4 = (bf16[8,8192]{1,0:T(8,128)(2,1)S(1)}, bf16[8,8192]{1,0:T(8,128)(2,1)S(1)}, u32[]{:S(2)}, u32[]{:S(2)}) collective-permute-start(bf16[8,8192]{1,0:T(8,128)(2,1)S(1)} %get-tuple-element.55), channel_id=1, source_target_pairs={{0,7},{1,0},{2,1},{3,2},{4,3},{5,4},{6,5},{7,6},{8,15},{9,8},{10,9... | collective-permute-start | bytes 393224 | tf_op jit(solution)/shard_map/ppermute | solution.py:30
  12.5 4.5 %shard_map.104 = (bf16[2,4,128,256]{3,2,1,0:T(8,128)(2,1)}, bf16[2,4,128,256]{3,2,1,0:T(8,128)(2,1)}, bf16[2,4,128,256]{3,2,1,0:T(8,128)(2,1)}, bf16[2,4,128,256]{3,2,1,0:T(8,128)(2,1)}) custom-call(s32[4]{0:T(128)} %fusion.6.order_ref, s32[3]{0:T(128)} %pad_add_fusion.place_ref, bf16[4,128,2048]{2,1,0:T(8,128)(2,1)} %bitcast.35), custom_call_target="tpu_custom_call" | custom-call | tf_op jit(solution)/shard_map/pallas_call | solution.py:48
  26.9 2.7 %collective-permute-start.6 = (bf16[8,8192]{1,0:T(8,128)(2,1)S(1)}, bf16[8,8192]{1,0:T(8,128)(2,1)S(1)}, u32[]{:S(2)}, u32[]{:S(2)}) collective-permute-start(bf16[8,8192]{1,0:T(8,128)(2,1)S(1)} %collective-permute-done.4), channel_id=1, source_target_pairs={{0,7},{1,0},{2,1},{3,2},{4,3},{5,4},{6,5},{7,6},{8,15},{9,8},{10,9... | collective-permute-start | bytes 393224 | tf_op jit(solution)/shard_map/ppermute | solution.py:30
  32.3 2.7 %collective-permute-start.8 = (bf16[8,8192]{1,0:T(8,128)(2,1)S(1)}, bf16[8,8192]{1,0:T(8,128)(2,1)S(1)}, u32[]{:S(2)}, u32[]{:S(2)}) collective-permute-start(bf16[8,8192]{1,0:T(8,128)(2,1)S(1)} %collective-permute-done.6), channel_id=1, source_target_pairs={{0,7},{1,0},{2,1},{3,2},{4,3},{5,4},{6,5},{7,6},{8,15},{9,8},{10,9... | collective-permute-start | bytes 393224 | tf_op jit(solution)/shard_map/ppermute | solution.py:30
  37.0 3.5 %collective-permute-start.10 = (bf16[8,4096]{1,0:T(8,128)(2,1)S(1)}, bf16[8,4096]{1,0:T(8,128)(2,1)S(1)}, u32[]{:S(2)}, u32[]{:S(2)}) collective-permute-start(bf16[8,4096]{1,0:T(8,128)(2,1)S(1)} %slice.41), channel_id=1, source_target_pairs={{0,7},{1,0},{2,1},{3,2},{4,3},{5,4},{6,5},{7,6},{8,15},{9,8},{10,9... | collective-permute-start | bytes 196616 | tf_op jit(solution)/shard_map/ppermute | solution.py:30
  41.8 3.2 %collective-permute-done.9 = bf16[8,4096]{1,0:T(8,128)(2,1)S(1)} collective-permute-done((bf16[8,4096]{1,0:T(8,128)(2,1)S(1)}, bf16[8,4096]{1,0:T(8,128)(2,1)S(1)}, u32[]{:S(2)}, u32[]{:S(2)}) %collective-permute-start.9) | collective-permute-done | bytes 65568 | tf_op jit(solution)/shard_map/ppermute | solution.py:30
  45.0 3.3 %pad_maximum_fusion.1 = bf16[8,4,128,256]{3,2,1,0:T(8,128)(2,1)} fusion(bf16[8,1,128,256]{3,2,1,0:T(8,128)(2,1)} %bitcast.19, bf16[8,1,128,256]{3,2,1,0:T(8,128)(2,1)} %bitcast.18, bf16[8,1,128,256]{3,2,1,0:T(8,128)(2,1)} %bitcast.17, bf16[8,1,128,256]{3,2,1,0:T(8,128)(2,1)S(1)} %bitcast.36), kind=kLoop, calls=%fused_computation.1 | loop fusion | flops 3145728 | bytes 4194304 | tf_op jit(solution)/shard_map/stack | solution.py:334
  48.3 5.2 %all-to-all-start = ((bf16[8,4,128,256]{3,2,1,0:T(8,128)(2,1)}), bf16[8,4,128,256]{3,2,1,0:T(8,128)(2,1)}, u32[]{:S(2)}, u32[]{:S(2)}) async-start(bf16[8,4,128,256]{3,2,1,0:T(8,128)(2,1)} %pad_maximum_fusion.1), calls=%async_computation | async-start | bytes 4194304 | tf_op jit(solution)/shard_map/all_to_all | solution.py:334
  59.1 15.3 %collective-permute-done.11.x1 = bf16[64,8192]{1,0:T(8,128)(2,1)S(1)} collective-permute-done((bf16[64,8192]{1,0:T(8,128)(2,1)S(1)}, bf16[64,8192]{1,0:T(8,128)(2,1)S(1)}, u32[]{:S(2)}, u32[]{:S(2)}) %collective-permute-start.11) | collective-permute-done | bytes 1048608 | tf_op jit(solution)/shard_map/ppermute | solution.py:30
  74.6 2.7 %collective-permute-start.14 = (bf16[32,8192]{1,0:T(8,128)(2,1)S(1)}, bf16[32,8192]{1,0:T(8,128)(2,1)S(1)}, u32[]{:S(2)}, u32[]{:S(2)}) collective-permute-start(bf16[32,8192]{1,0:T(8,128)(2,1)S(1)} %slice.43), channel_id=1, source_target_pairs={{0,24},{8,0},{16,8},{24,16},{1,25},{9,1},{17,9},{25,17},{2,26},{10... | collective-permute-start | bytes 1572872 | tf_op jit(solution)/shard_map/ppermute | solution.py:30
  79.5 6.5 %collective-permute-done.13.x3a = bf16[32,8192]{1,0:T(8,128)(2,1)S(1)} collective-permute-done((bf16[32,8192]{1,0:T(8,128)(2,1)S(1)}, bf16[32,8192]{1,0:T(8,128)(2,1)S(1)}, u32[]{:S(2)}, u32[]{:S(2)}) %collective-permute-start.13) | collective-permute-done | bytes 524320 | tf_op jit(solution)/shard_map/ppermute | solution.py:30
  86.9 10.0 %shard_map.105 = (bf16[64,384]{1,0:T(8,128)(2,1)}, bf16[64,384]{1,0:T(8,128)(2,1)}, bf16[64,384]{1,0:T(8,128)(2,1)}, bf16[64,384]{1,0:T(8,128)(2,1)}) custom-call(s32[3]{0:T(128)} %pad_add_fusion.place_ref, bf16[64,8192]{1,0:T(8,128)(2,1)} %copy-done.2, bf16[64,8192]{1,0:T(8,128)(2,1)} %copy-done, bf16[64,8192]{1,0:T(8,128)(2,1)} %copy-done.1, ...), custom_call_target="tpu_custom_call" | custom-call | tf_op jit(solution)/shard_map/pallas_call | solution.py:126
  106.2 8.4 %shard_map.106 = (bf16[64,256]{1,0:T(8,128)(2,1)}, bf16[64,256]{1,0:T(8,128)(2,1)}, bf16[64,256]{1,0:T(8,128)(2,1)}, bf16[64,256]{1,0:T(8,128)(2,1)}, bf16[8,2048]{1,0:T(8,128)(2,1)}) custom-call(s32[34]{0:T(128)} %pad_add_fusion.1.info_ref, bf16[64,384]{1,0:T(8,128)(2,1)} %get-tuple-element.33.p0, bf16[64,384]{1,0:T(8,128)(2,1)} %copy-done.18, ...), custom_call_target="tpu_custom_call" | custom-call | tf_op jit(solution)/shard_map/pallas_call | solution.py:216
  121.5 3.8 %shard_map.109 = (bf16[64,4096]{1,0:T(8,128)(2,1)}, bf16[64,4096]{1,0:T(8,128)(2,1)}, bf16[64,4096]{1,0:T(8,128)(2,1)}, bf16[64,4096]{1,0:T(8,128)(2,1)}) custom-call(s32[3]{0:T(128)} %pad_add_fusion.place_ref, bf16[64,256]{1,0:T(8,128)(2,1)} %get-tuple-element.41.a0, bf16[64,256]{1,0:T(8,128)(2,1)} %copy-done.15, bf16[64,256]{1,0:T(8,128)(2,1)} %copy-done.16, ...), custom_call_target="tpu_custom_call" | custom-call | tf_op jit(solution)/shard_map/pallas_call | solution.py:249
  129.1 3.8 %shard_map.107 = (bf16[64,4096]{1,0:T(8,128)(2,1)}, bf16[64,4096]{1,0:T(8,128)(2,1)}, bf16[64,4096]{1,0:T(8,128)(2,1)}, bf16[64,4096]{1,0:T(8,128)(2,1)}) custom-call(s32[3]{0:T(128)} %pad_add_fusion.place_ref, bf16[64,256]{1,0:T(8,128)(2,1)} %get-tuple-element.41.a0, bf16[64,256]{1,0:T(8,128)(2,1)} %copy-done.15, bf16[64,256]{1,0:T(8,128)(2,1)} %copy-done.16, ...), custom_call_target="tpu_custom_call" | custom-call | tf_op jit(solution)/shard_map/pallas_call | solution.py:249
  134.2 2.7 %collective-permute-start.23 = (bf16[64,2048]{1,0:T(8,128)(2,1)S(1)}, bf16[64,2048]{1,0:T(8,128)(2,1)S(1)}, u32[]{:S(2)}, u32[]{:S(2)}) collective-permute-start(bf16[64,2048]{1,0:T(8,128)(2,1)S(1)} %get-tuple-element.58), channel_id=1, source_target_pairs={{0,24},{8,0},{16,8},{24,16},{1,25},{9,1},{17,9},{25,17},{2,26},{10... | collective-permute-start | bytes 786440 | tf_op jit(solution)/shard_map/ppermute | solution.py:30
  137.1 2.7 %collective-permute-start.31 = (bf16[64,4096]{1,0:T(8,128)(2,1)S(1)}, bf16[64,4096]{1,0:T(8,128)(2,1)S(1)}, u32[]{:S(2)}, u32[]{:S(2)}) collective-permute-start(bf16[64,4096]{1,0:T(8,128)(2,1)S(1)} %add_convert_fusion), channel_id=1, source_target_pairs={{0,24},{8,0},{16,8},{24,16},{1,25},{9,1},{17,9},{25,17},{2,26},{10... | collective-permute-start | bytes 1572872 | tf_op jit(solution)/shard_map/ppermute | solution.py:30
  140.8 8.6 %collective-permute-done.29.b1 = bf16[64,4096]{1,0:T(8,128)(2,1)S(1)} collective-permute-done((bf16[64,4096]{1,0:T(8,128)(2,1)S(1)}, bf16[64,4096]{1,0:T(8,128)(2,1)S(1)}, u32[]{:S(2)}, u32[]{:S(2)}) %collective-permute-start.29) | collective-permute-done | bytes 524320 | tf_op jit(solution)/shard_map/ppermute | solution.py:30
  152.7 4.5 %all-to-all-start.2 = ((bf16[8,8,4096]{2,1,0:T(8,128)(2,1)}), bf16[8,8,4096]{2,1,0:T(8,128)(2,1)S(1)}, u32[]{:S(2)}, u32[]{:S(2)}) async-start(bf16[8,8,4096]{2,1,0:T(8,128)(2,1)} %shard_map.110), calls=%async_computation.2 | async-start | bytes 1048576 | tf_op jit(solution)/shard_map/all_to_all | solution.py:377
  157.3 2.7 %collective-permute-start.24 = (bf16[64,4096]{1,0:T(8,128)(2,1)S(1)}, bf16[64,4096]{1,0:T(8,128)(2,1)S(1)}, u32[]{:S(2)}, u32[]{:S(2)}) collective-permute-start(bf16[64,4096]{1,0:T(8,128)(2,1)S(1)} %add_convert_fusion.2), channel_id=1, source_target_pairs={{0,24},{8,0},{16,8},{24,16},{1,25},{9,1},{17,9},{25,17},{2,26},{10... | collective-permute-start | bytes 1572872 | tf_op jit(solution)/shard_map/ppermute | solution.py:30
  167.9 2.7 %shard_map.108 = bf16[8,8,6144]{2,1,0:T(8,128)(2,1)} custom-call(s32[8]{0:T(128)} %and_select_fusion.5.pick_ref, bf16[64,4096]{1,0:T(8,128)(2,1)} %get-tuple-element.45.b0, bf16[64,4096]{1,0:T(8,128)(2,1)} %copy-done.12, bf16[64,4096]{1,0:T(8,128)(2,1)} %copy-done.13, bf16[8,2048]{1,0:T(8,128)(2,1)} %get-tuple-element.49.rest_0_, ...), custom_call_target="tpu_custom_call" | custom-call | tf_op jit(solution)/shard_map/pallas_call | solution.py:281
  170.5 6.8 %all-to-all-start.1 = ((bf16[8,8,6144]{2,1,0:T(8,128)(2,1)}), bf16[8,8,6144]{2,1,0:T(8,128)(2,1)S(1)}, u32[]{:S(2)}, u32[]{:S(2)}) async-start(bf16[8,8,6144]{2,1,0:T(8,128)(2,1)} %shard_map.108), calls=%async_computation.1 | async-start | bytes 1572864 | tf_op jit(solution)/shard_map/all_to_all | solution.py:377
  179.9 13.3 %all-to-all-done.1 = bf16[8,8,6144]{2,1,0:T(8,128)(2,1)S(1)} async-done(((bf16[8,8,6144]{2,1,0:T(8,128)(2,1)}), bf16[8,8,6144]{2,1,0:T(8,128)(2,1)S(1)}, u32[]{:S(2)}, u32[]{:S(2)}) %all-to-all-start.1) | async-done | bytes 786464 | tf_op jit(solution)/shard_map/all_to_all | solution.py:377
  193.4 17.3 %collective-permute-start.32 = (bf16[8,8192]{1,0:T(8,128)(2,1)S(1)}, bf16[8,8192]{1,0:T(8,128)(2,1)S(1)}, u32[]{:S(2)}, u32[]{:S(2)}) collective-permute-start(bf16[8,8192]{1,0:T(8,128)(2,1)S(1)} %fusion.3), channel_id=1, source_target_pairs={{0,32},{32,64},{64,96},{96,128},{128,160},{160,192},{192,224},{224... | collective-permute-start | bytes 393224 | tf_op jit(solution)/shard_map/ppermute | solution.py:30
  (158 shorter events, 68.7 us)
Async XLA Ops:
  2.8 24.0 %collective-permute-start.3 = (bf16[8,8192]{1,0:T(8,128)(2,1)S(1)}, bf16[8,8192]{1,0:T(8,128)(2,1)S(1)}, u32[]{:S(2)}, u32[]{:S(2)}) collective-permute-start(bf16[8,8192]{1,0:T(8,128)(2,1)S(1)} %get-tuple-element.55), channel_id=1, source_target_pairs={{0,1},{1,2},{2,3},{3,4},{4,5},{5,6},{6,7},{7,0},{8,9},{9,10},{10,1... | collective-permute-start | bytes 393224 | tf_op jit(solution)/shard_map/ppermute | solution.py:30
  5.3 21.5 %collective-permute-start.4 = (bf16[8,8192]{1,0:T(8,128)(2,1)S(1)}, bf16[8,8192]{1,0:T(8,128)(2,1)S(1)}, u32[]{:S(2)}, u32[]{:S(2)}) collective-permute-start(bf16[8,8192]{1,0:T(8,128)(2,1)S(1)} %get-tuple-element.55), channel_id=1, source_target_pairs={{0,7},{1,0},{2,1},{3,2},{4,3},{5,4},{6,5},{7,6},{8,15},{9,8},{10,9... | collective-permute-start | bytes 393224 | tf_op jit(solution)/shard_map/ppermute | solution.py:30
  17.0 28.0 %collective-permute-start = (bf16[8,128,256]{2,1,0:T(8,128)(2,1)}, bf16[8,128,256]{2,1,0:T(8,128)(2,1)}, u32[]{:S(2)}, u32[]{:S(2)}) collective-permute-start(bf16[8,128,256]{2,1,0:T(8,128)(2,1)} %bitcast.43), channel_id=1, source_target_pairs={{0,8},{8,16},{16,24},{24,0},{1,9},{9,17},{17,25},{25,1},{2,10},{10... | collective-permute-start | bytes 1572872 | tf_op jit(solution)/shard_map/ppermute | solution.py:30
  18.3 26.7 %collective-permute-start.1 = (bf16[8,128,256]{2,1,0:T(8,128)(2,1)}, bf16[8,128,256]{2,1,0:T(8,128)(2,1)}, u32[]{:S(2)}, u32[]{:S(2)}) collective-permute-start(bf16[8,128,256]{2,1,0:T(8,128)(2,1)} %bitcast.42), channel_id=1, source_target_pairs={{0,16},{8,24},{16,0},{24,8},{1,17},{9,25},{17,1},{25,9},{2,18},{10... | collective-permute-start | bytes 1572872 | tf_op jit(solution)/shard_map/ppermute | solution.py:30
  20.9 24.1 %collective-permute-start.2 = (bf16[8,128,256]{2,1,0:T(8,128)(2,1)}, bf16[8,128,256]{2,1,0:T(8,128)(2,1)}, u32[]{:S(2)}, u32[]{:S(2)}) collective-permute-start(bf16[8,128,256]{2,1,0:T(8,128)(2,1)} %bitcast.41), channel_id=1, source_target_pairs={{0,24},{8,0},{16,8},{24,16},{1,25},{9,1},{17,9},{25,17},{2,26},{10... | collective-permute-start | bytes 1572872 | tf_op jit(solution)/shard_map/ppermute | solution.py:30
  32.2 8.2 %collective-permute-start.7 = (bf16[8,8192]{1,0:T(8,128)(2,1)S(1)}, bf16[8,8192]{1,0:T(8,128)(2,1)S(1)}, u32[]{:S(2)}, u32[]{:S(2)}) collective-permute-start(bf16[8,8192]{1,0:T(8,128)(2,1)S(1)} %collective-permute-done.5), channel_id=1, source_target_pairs={{0,1},{1,2},{2,3},{3,4},{4,5},{5,6},{6,7},{7,0},{8,9},{9,10},{10,1... | collective-permute-start | bytes 393224 | tf_op jit(solution)/shard_map/ppermute | solution.py:30
  48.3 57.2 %all-to-all-start = ((bf16[8,4,128,256]{3,2,1,0:T(8,128)(2,1)}), bf16[8,4,128,256]{3,2,1,0:T(8,128)(2,1)}, u32[]{:S(2)}, u32[]{:S(2)}) async-start(bf16[8,4,128,256]{3,2,1,0:T(8,128)(2,1)} %pad_maximum_fusion.1), calls=%async_computation | async-start | bytes 4194304 | tf_op jit(solution)/shard_map/all_to_all | solution.py:334
  53.8 20.6 %collective-permute-start.11 = (bf16[64,8192]{1,0:T(8,128)(2,1)S(1)}, bf16[64,8192]{1,0:T(8,128)(2,1)S(1)}, u32[]{:S(2)}, u32[]{:S(2)}) collective-permute-start(bf16[64,8192]{1,0:T(8,128)(2,1)S(1)} %maximum_dynamic-update-slice_fusion.x0), channel_id=1, source_target_pairs={{0,8},{8,16},{16,24},{24,0},{1,9},{9,17},{17,25},{25,1},{2,10},{10... | collective-permute-start | bytes 3145736 | tf_op jit(solution)/shard_map/ppermute | solution.py:30
  53.9 20.6 %collective-permute-start.12 = (bf16[64,8192]{1,0:T(8,128)(2,1)S(1)}, bf16[64,8192]{1,0:T(8,128)(2,1)S(1)}, u32[]{:S(2)}, u32[]{:S(2)}) collective-permute-start(bf16[64,8192]{1,0:T(8,128)(2,1)S(1)} %maximum_dynamic-update-slice_fusion.x0), channel_id=1, source_target_pairs={{0,24},{8,0},{16,8},{24,16},{1,25},{9,1},{17,9},{25,17},{2,26},{10... | collective-permute-start | bytes 3145736 | tf_op jit(solution)/shard_map/ppermute | solution.py:30
  74.4 11.6 %collective-permute-start.13 = (bf16[32,8192]{1,0:T(8,128)(2,1)S(1)}, bf16[32,8192]{1,0:T(8,128)(2,1)S(1)}, u32[]{:S(2)}, u32[]{:S(2)}) collective-permute-start(bf16[32,8192]{1,0:T(8,128)(2,1)S(1)} %slice.42), channel_id=1, source_target_pairs={{0,8},{8,16},{16,24},{24,0},{1,9},{9,17},{17,25},{25,1},{2,10},{10... | collective-permute-start | bytes 1572872 | tf_op jit(solution)/shard_map/ppermute | solution.py:30
  74.6 11.4 %collective-permute-start.14 = (bf16[32,8192]{1,0:T(8,128)(2,1)S(1)}, bf16[32,8192]{1,0:T(8,128)(2,1)S(1)}, u32[]{:S(2)}, u32[]{:S(2)}) collective-permute-start(bf16[32,8192]{1,0:T(8,128)(2,1)S(1)} %slice.43), channel_id=1, source_target_pairs={{0,24},{8,0},{16,8},{24,16},{1,25},{9,1},{17,9},{25,17},{2,26},{10... | collective-permute-start | bytes 1572872 | tf_op jit(solution)/shard_map/ppermute | solution.py:30
  97.0 6.0 %collective-permute-start.15 = (bf16[64,384]{1,0:T(8,128)(2,1)}, bf16[64,384]{1,0:T(8,128)(2,1)S(1)}, u32[]{:S(2)}, u32[]{:S(2)}) collective-permute-start(bf16[64,384]{1,0:T(8,128)(2,1)} %get-tuple-element.34), channel_id=1, source_target_pairs={{0,1},{1,2},{2,3},{3,0},{4,5},{5,6},{6,7},{7,4},{8,9},{9,10},{10,1... | collective-permute-start | bytes 147464 | tf_op jit(solution)/shard_map/ppermute | solution.py:35
  98.1 7.4 %collective-permute-start.16 = (bf16[64,384]{1,0:T(8,128)(2,1)}, bf16[64,384]{1,0:T(8,128)(2,1)S(1)}, u32[]{:S(2)}, u32[]{:S(2)}) collective-permute-start(bf16[64,384]{1,0:T(8,128)(2,1)} %get-tuple-element.35), channel_id=1, source_target_pairs={{0,2},{1,3},{2,0},{3,1},{4,6},{5,7},{6,4},{7,5},{8,10},{9,11},{10,... | collective-permute-start | bytes 147464 | tf_op jit(solution)/shard_map/ppermute | solution.py:35
  126.4 10.5 %collective-permute-start.28 = (bf16[64,2048]{1,0:T(8,128)(2,1)S(1)}, bf16[64,2048]{1,0:T(8,128)(2,1)S(1)}, u32[]{:S(2)}, u32[]{:S(2)}) collective-permute-start(bf16[64,2048]{1,0:T(8,128)(2,1)S(1)} %get-tuple-element.61), channel_id=1, source_target_pairs={{0,8},{8,16},{16,24},{24,0},{1,9},{9,17},{17,25},{25,1},{2,10},{10... | collective-permute-start | bytes 786440 | tf_op jit(solution)/shard_map/ppermute | solution.py:30
  126.5 10.5 %collective-permute-start.30 = (bf16[64,2048]{1,0:T(8,128)(2,1)S(1)}, bf16[64,2048]{1,0:T(8,128)(2,1)S(1)}, u32[]{:S(2)}, u32[]{:S(2)}) collective-permute-start(bf16[64,2048]{1,0:T(8,128)(2,1)S(1)} %get-tuple-element.60), channel_id=1, source_target_pairs={{0,24},{8,0},{16,8},{24,16},{1,25},{9,1},{17,9},{25,17},{2,26},{10... | collective-permute-start | bytes 786440 | tf_op jit(solution)/shard_map/ppermute | solution.py:30
  134.1 6.5 %collective-permute-start.21 = (bf16[64,2048]{1,0:T(8,128)(2,1)S(1)}, bf16[64,2048]{1,0:T(8,128)(2,1)S(1)}, u32[]{:S(2)}, u32[]{:S(2)}) collective-permute-start(bf16[64,2048]{1,0:T(8,128)(2,1)S(1)} %get-tuple-element.59), channel_id=1, source_target_pairs={{0,8},{8,16},{16,24},{24,0},{1,9},{9,17},{17,25},{25,1},{2,10},{10... | collective-permute-start | bytes 786440 | tf_op jit(solution)/shard_map/ppermute | solution.py:30
  134.2 23.0 %collective-permute-start.23 = (bf16[64,2048]{1,0:T(8,128)(2,1)S(1)}, bf16[64,2048]{1,0:T(8,128)(2,1)S(1)}, u32[]{:S(2)}, u32[]{:S(2)}) collective-permute-start(bf16[64,2048]{1,0:T(8,128)(2,1)S(1)} %get-tuple-element.58), channel_id=1, source_target_pairs={{0,24},{8,0},{16,8},{24,16},{1,25},{9,1},{17,9},{25,17},{2,26},{10... | collective-permute-start | bytes 786440 | tf_op jit(solution)/shard_map/ppermute | solution.py:30
  136.9 12.4 %collective-permute-start.29 = (bf16[64,4096]{1,0:T(8,128)(2,1)S(1)}, bf16[64,4096]{1,0:T(8,128)(2,1)S(1)}, u32[]{:S(2)}, u32[]{:S(2)}) collective-permute-start(bf16[64,4096]{1,0:T(8,128)(2,1)S(1)} %add_convert_fusion.1), channel_id=1, source_target_pairs={{0,8},{8,16},{16,24},{24,0},{1,9},{9,17},{17,25},{25,1},{2,10},{10... | collective-permute-start | bytes 1572872 | tf_op jit(solution)/shard_map/ppermute | solution.py:30
  137.1 12.2 %collective-permute-start.31 = (bf16[64,4096]{1,0:T(8,128)(2,1)S(1)}, bf16[64,4096]{1,0:T(8,128)(2,1)S(1)}, u32[]{:S(2)}, u32[]{:S(2)}) collective-permute-start(bf16[64,4096]{1,0:T(8,128)(2,1)S(1)} %add_convert_fusion), channel_id=1, source_target_pairs={{0,24},{8,0},{16,8},{24,16},{1,25},{9,1},{17,9},{25,17},{2,26},{10... | collective-permute-start | bytes 1572872 | tf_op jit(solution)/shard_map/ppermute | solution.py:30
  140.7 26.2 %collective-permute-start.22 = (bf16[64,4096]{1,0:T(8,128)(2,1)S(1)}, bf16[64,4096]{1,0:T(8,128)(2,1)S(1)}, u32[]{:S(2)}, u32[]{:S(2)}) collective-permute-start(bf16[64,4096]{1,0:T(8,128)(2,1)S(1)} %add_convert_fusion.3), channel_id=1, source_target_pairs={{0,8},{8,16},{16,24},{24,0},{1,9},{9,17},{17,25},{25,1},{2,10},{10... | collective-permute-start | bytes 1572872 | tf_op jit(solution)/shard_map/ppermute | solution.py:30
  152.7 17.8 %all-to-all-start.2 = ((bf16[8,8,4096]{2,1,0:T(8,128)(2,1)}), bf16[8,8,4096]{2,1,0:T(8,128)(2,1)S(1)}, u32[]{:S(2)}, u32[]{:S(2)}) async-start(bf16[8,8,4096]{2,1,0:T(8,128)(2,1)} %shard_map.110), calls=%async_computation.2 | async-start | bytes 1048576 | tf_op jit(solution)/shard_map/all_to_all | solution.py:377
  157.3 9.6 %collective-permute-start.24 = (bf16[64,4096]{1,0:T(8,128)(2,1)S(1)}, bf16[64,4096]{1,0:T(8,128)(2,1)S(1)}, u32[]{:S(2)}, u32[]{:S(2)}) collective-permute-start(bf16[64,4096]{1,0:T(8,128)(2,1)S(1)} %add_convert_fusion.2), channel_id=1, source_target_pairs={{0,24},{8,0},{16,8},{24,16},{1,25},{9,1},{17,9},{25,17},{2,26},{10... | collective-permute-start | bytes 1572872 | tf_op jit(solution)/shard_map/ppermute | solution.py:30
  170.5 22.7 %all-to-all-start.1 = ((bf16[8,8,6144]{2,1,0:T(8,128)(2,1)}), bf16[8,8,6144]{2,1,0:T(8,128)(2,1)S(1)}, u32[]{:S(2)}, u32[]{:S(2)}) async-start(bf16[8,8,6144]{2,1,0:T(8,128)(2,1)} %shard_map.108), calls=%async_computation.1 | async-start | bytes 1572864 | tf_op jit(solution)/shard_map/all_to_all | solution.py:377
  193.4 19.3 %collective-permute-start.32 = (bf16[8,8192]{1,0:T(8,128)(2,1)S(1)}, bf16[8,8192]{1,0:T(8,128)(2,1)S(1)}, u32[]{:S(2)}, u32[]{:S(2)}) collective-permute-start(bf16[8,8192]{1,0:T(8,128)(2,1)S(1)} %fusion.3), channel_id=1, source_target_pairs={{0,32},{32,64},{64,96},{96,128},{128,160},{160,192},{192,224},{224... | collective-permute-start | bytes 393224 | tf_op jit(solution)/shard_map/ppermute | solution.py:30
  (40 other events, 248.2 us)
